TPU v7x, 512 devices: a whole 4x4x16 slice. The times are simulated.
512 devices in a mesh: row: 64 (over y_lo, z, core), col: 8 (over x, y_hi).
Axes of the slice: x: 4, y: 4 (y_hi: 2, y_lo: 2; y = y_hi * 2 + y_lo), z: 16, core: 2. Of those that a mesh axis runs over, the one named last changes fastest.
Arguments:
- x_tiles: bfloat16 [192, 32, 128, 128], P('row', 'col'), may hold values from -0.59765625 to 0.59765625
- tile_cols: int32 [192, 32], P('row', 'col'), may hold values from 0 to 191, as said below
- tile_counts: int32 [192, 8], P('row', 'col'), may hold values from 1 to 4
Outputs:
- product: bfloat16 [192, 32, 128, 128], P('row', 'col')
Inputs may be any that keep to these rules, and one draw needn't show every extreme that they name: `tile_cols`: in block row i the slots p * 4 to (p + 1) * 4 - 1 hold 4 distinct block columns of panel p, each of the form p * 24 + ((i + d) mod 24) with -2 <= d <= 2.
All inputs are finite; a program needn't handle non-finite values.
Results may differ from a plain program's by a relative error of at most 0.001.
Values may be sent and summed in bfloat16 or wider, within the bound.
No kernel may reach another device: no remote copies, remote signals or barrier semaphores. Data moves between devices by JAX's collectives and lax.ppermute only.
A program may use at most 128 MiB of HBM per device.

v0:
```python
import jax
import jax.numpy as jnp
from jax import lax
from jax.sharding import PartitionSpec as P

PANELS = 8
PS = 4


def from_behind(block, axis, distance):
    devices = range(lax.axis_size(axis))
    route = [((i - distance) % len(devices), i) for i in devices]
    return lax.ppermute(block, axis, route)


def slot_live(tile_cols, tile_counts):
    repeated = jnp.repeat(tile_counts, PS, axis=1)
    position = lax.broadcasted_iota(jnp.int32, tile_cols.shape, 1) % PS
    return position < repeated


def body(x_tiles, tile_cols, tile_counts):
    rows_here = tile_cols.shape[0]
    count_row = lax.axis_size("row")
    here = lax.axis_index("row")
    stride = count_row // PANELS
    zero_tile = jnp.zeros((), x_tiles.dtype)
    own_live = slot_live(tile_cols, tile_counts)
    left_tiles, left_cols, left_counts = (
        lax.all_gather(x_tiles, "col", axis=1, tiled=True),
        lax.all_gather(tile_cols, "col", axis=1, tiled=True),
        lax.all_gather(tile_counts, "col", axis=1, tiled=True),
    )
    left_keyed = jnp.where(slot_live(left_cols, left_counts), left_cols, -1).astype(jnp.int32)
    block = (x_tiles, tile_cols, tile_counts)
    local_span = jnp.arange(rows_here, dtype=jnp.int32)
    offsets = sorted(
        set(((p * stride + e) % count_row for p in range(PANELS) for e in (-1, 0, 1))) - {0}
    )
    pieces = [block]
    id_list = [here * rows_here + local_span]
    for offset in offsets:
        moved = from_behind((block[0], block[1], block[2]), "row", count_row - offset)
        pieces.append(moved)
        id_list.append((here + offset) % count_row * rows_here + local_span)
    stack_tiles = jnp.concatenate([piece[0] for piece in pieces], axis=0)
    stack_cols = jnp.concatenate([piece[1] for piece in pieces], axis=0)
    stack_counts = jnp.concatenate([piece[2] for piece in pieces], axis=0)
    stack_ids = jnp.concatenate(id_list, axis=0).astype(jnp.int32)
    stack_keyed = jnp.where(slot_live(stack_cols, stack_counts), stack_cols, -1).astype(jnp.int32)
    position = jnp.arange(stack_ids.shape[0], dtype=jnp.int32)
    earlier = (stack_ids[:, None] == stack_ids[None, :]) & (position[:, None] > position[None, :])
    unique_row = jnp.logical_not(jnp.any(earlier, axis=1))
    group = 2 * PS
    turns = left_cols.shape[1] // group

    def advance(accum, index):
        first = index * group
        part_tiles = lax.dynamic_slice_in_dim(left_tiles, first, group, 1)
        part_keyed = lax.dynamic_slice_in_dim(left_keyed, first, group, 1)
        part_tiles = jnp.where((part_keyed >= 0)[:, :, None, None], part_tiles, zero_tile)
        matches = (part_keyed[:, :, None] == stack_ids[None, None, :]) & unique_row[None, None, :]
        chosen = jnp.einsum(
            "rgf,fuxy->rguxy",
            matches.astype(jnp.bfloat16),
            stack_tiles,
            preferred_element_type=jnp.float32,
        ).astype(jnp.bfloat16)
        chosen_cols = jnp.sum(
            jnp.where(matches[:, :, :, None], stack_keyed[None, None, :, :], 0), axis=2
        )
        hits = (chosen_cols[:, :, :, None] == tile_cols[:, None, None, :]).astype(jnp.bfloat16)
        placed = jnp.einsum(
            "rgus,rguxy->rgsxy", hits, chosen, preferred_element_type=jnp.float32
        ).astype(jnp.bfloat16)
        accum = accum + jnp.einsum(
            "rgxy,rgsyz->rsxz", part_tiles, placed, preferred_element_type=jnp.float32
        )
        return (accum, None)

    initial = jnp.zeros(
        (rows_here, tile_cols.shape[1], x_tiles.shape[-1], x_tiles.shape[-1]), jnp.float32
    )
    summed, _ = lax.scan(advance, initial, jnp.arange(turns, dtype=jnp.int32))
    return jnp.where(own_live[:, :, None, None], summed, 0.0).astype(jnp.bfloat16)


def solution(mesh):
    placed = (P("row", "col", None, None), P("row", "col"), P("row", "col"))
    return jax.shard_map(
        body, mesh=mesh, in_specs=placed, out_specs=P("row", "col", None, None), check_vma=False
    )
```

profile of v0, /device:TPU:80, one launch (start us, length us, event | category | flops | bytes accessed | tf_op | source)
XLA Modules:
  0.0 1222.7 jit_solution(1086816939266158125)
XLA Ops:
  9.2 11.8 collective-permute-start.1
  24.8 5.0 collective-permute-start.47
  45.3 45.1 %collective-permute-done.12 = s32[3,1]{0,1:T(1,128)S(1)} collective-permute-done((s32[3,1]{0,1:T(1,128)}, s32[3,1]{0,1:T(1,128)S(1)}, u32[]{:S(2)}, u32[]{:S(2)}) %collective-permute-start.12) | collective-permute-done | bytes 44 | tf_op jit(solution)/shard_map/ppermute | solution.py:13
  94.8 10.3 collective-permute-done.13
  105.1 5.6 collective-permute-start.15
  112.7 5.2 collective-permute-done.15
  117.9 11.5 collective-permute-start.17
  129.4 11.3 collective-permute-start.18
  144.0 7.8 collective-permute-start.2
  155.8 8.8 collective-permute-start.21
  164.6 6.6 collective-permute-start.22
  171.5 4.9 collective-permute-start.3
  176.5 5.5 collective-permute-start.4
  182.0 8.7 collective-permute-start.5
  190.7 8.1 collective-permute-start.6
  204.4 5.9 collective-permute-start.8
  210.4 5.0 collective-permute-start.9
  215.5 4.5 collective-permute-start.23
  220.0 5.2 collective-permute-start.24
  225.2 5.7 collective-permute-start.25
  230.9 4.5 collective-permute-start.26
  235.5 8.7 collective-permute-start.27
  244.3 9.1 collective-permute-start.28
  253.4 5.7 collective-permute-start.29
  259.1 5.6 collective-permute-start.30
  285.4 6.7 collective-permute-start.36
  292.2 5.2 collective-permute-start.37
  302.4 7.4 collective-permute-start.39
  309.9 7.2 collective-permute-start.40
  317.1 5.8 collective-permute-start.41
  331.7 5.2 collective-permute-start.43
  348.6 8.7 collective-permute-start.50
  357.3 8.3 collective-permute-start.51
  365.6 5.1 collective-permute-start.52
  370.7 5.7 collective-permute-start.53
  378.7 27.4 %collective-permute-done.49 = bf16[3,4,128,128]{3,0,2,1:T(4,128)(2,1)S(1)} collective-permute-done((bf16[3,4,128,128]{3,0,2,1:T(4,128)(2,1)S(1)}, bf16[3,4,128,128]{3,0,2,1:T(4,128)(2,1)S(1)}, u32[]{:S(2)}, u32[]{:S(2)}) %collective-permute-start.49) | collective-permute-done | bytes 393248 | tf_op jit(solution)/shard_map/ppermute | solution.py:13
  408.0 48.2 %collective-permute-done.50 = bf16[3,4,128,128]{3,0,2,1:T(4,128)(2,1)S(1)} collective-permute-done((bf16[3,4,128,128]{3,0,2,1:T(4,128)(2,1)S(1)}, bf16[3,4,128,128]{3,0,2,1:T(4,128)(2,1)S(1)}, u32[]{:S(2)}, u32[]{:S(2)}) %collective-permute-start.50) | collective-permute-done | bytes 393248 | tf_op jit(solution)/shard_map/ppermute | solution.py:13
  456.2 22.4 %collective-permute-start.55 = (bf16[3,4,128,128]{3,0,2,1:T(4,128)(2,1)S(1)}, bf16[3,4,128,128]{3,0,2,1:T(4,128)(2,1)}, u32[]{:S(2)}, u32[]{:S(2)}) collective-permute-start(bf16[3,4,128,128]{3,0,2,1:T(4,128)(2,1)S(1)} %copy.170), channel_id=1, source_target_pairs={{200,0},{208,8},{216,16},{224,24},{232,32},{240,40},{248,48},{256,... | collective-permute-start | bytes 1179656 | tf_op jit(solution)/shard_map/ppermute | solution.py:13
  480.6 29.5 %collective-permute-done.52 = bf16[3,4,128,128]{3,0,2,1:T(4,128)(2,1)S(1)} collective-permute-done((bf16[3,4,128,128]{3,0,2,1:T(4,128)(2,1)S(1)}, bf16[3,4,128,128]{3,0,2,1:T(4,128)(2,1)S(1)}, u32[]{:S(2)}, u32[]{:S(2)}) %collective-permute-start.52) | collective-permute-done | bytes 393248 | tf_op jit(solution)/shard_map/ppermute | solution.py:13
  512.0 38.5 %collective-permute-done.53 = bf16[3,4,128,128]{3,0,2,1:T(4,128)(2,1)S(1)} collective-permute-done((bf16[3,4,128,128]{3,0,2,1:T(4,128)(2,1)S(1)}, bf16[3,4,128,128]{3,0,2,1:T(4,128)(2,1)S(1)}, u32[]{:S(2)}, u32[]{:S(2)}) %collective-permute-start.53) | collective-permute-done | bytes 393248 | tf_op jit(solution)/shard_map/ppermute | solution.py:13
  550.5 52.7 %collective-permute-start.58 = (bf16[3,4,128,128]{3,0,2,1:T(4,128)(2,1)S(1)}, bf16[3,4,128,128]{3,0,2,1:T(4,128)(2,1)}, u32[]{:S(2)}, u32[]{:S(2)}) collective-permute-start(bf16[3,4,128,128]{3,0,2,1:T(4,128)(2,1)S(1)} %copy.170), channel_id=1, source_target_pairs={{264,0},{272,8},{280,16},{288,24},{296,32},{304,40},{312,48},{320,... | collective-permute-start | bytes 1179656 | tf_op jit(solution)/shard_map/ppermute | solution.py:13
  603.8 18.3 %all-gather = s32[8,1,3]{2,1,0:T(1,128)S(1)} all-gather(s32[1,1,3]{2,1,0:T(1,128)} %bitcast.55), channel_id=1, replica_groups=mesh['row'=64,'col'=8] {'col'}, dimensions={0}, use_global_device_ids=true | all-gather | bytes 108 | tf_op jit(solution)/shard_map/all_gather | solution.py:32
  623.9 30.9 %all-gather.1 = s32[8,4,3]{2,1,0:T(4,128)S(1)} all-gather(s32[1,4,3]{2,1,0:T(4,128)S(1)} %bitcast.53), channel_id=1, replica_groups=mesh['row'=64,'col'=8] {'col'}, dimensions={0}, use_global_device_ids=true | all-gather | bytes 432 | tf_op jit(solution)/shard_map/all_gather | solution.py:31
  657.0 6.8 collective-permute-start.60
  663.8 19.7 %collective-permute-start.61 = (bf16[3,4,128,128]{3,0,2,1:T(4,128)(2,1)S(1)}, bf16[3,4,128,128]{3,0,2,1:T(4,128)(2,1)S(1)}, u32[]{:S(2)}, u32[]{:S(2)}) collective-permute-start(bf16[3,4,128,128]{3,0,2,1:T(4,128)(2,1)S(1)} %copy.170), channel_id=1, source_target_pairs={{328,0},{336,8},{344,16},{352,24},{360,32},{368,40},{376,48},{384,... | collective-permute-start | bytes 1179656 | tf_op jit(solution)/shard_map/ppermute | solution.py:13
  687.7 42.4 %collective-permute-done.59 = bf16[3,4,128,128]{3,0,2,1:T(4,128)(2,1)S(1)} collective-permute-done((bf16[3,4,128,128]{3,0,2,1:T(4,128)(2,1)S(1)}, bf16[3,4,128,128]{3,0,2,1:T(4,128)(2,1)S(1)}, u32[]{:S(2)}, u32[]{:S(2)}) %collective-permute-start.59) | collective-permute-done | bytes 393248 | tf_op jit(solution)/shard_map/ppermute | solution.py:13
  730.1 11.8 collective-permute-start.64
  741.9 16.8 %collective-permute-start.65 = (bf16[3,4,128,128]{3,0,2,1:T(4,128)(2,1)S(1)}, bf16[3,4,128,128]{3,0,2,1:T(4,128)(2,1)}, u32[]{:S(2)}, u32[]{:S(2)}) collective-permute-start(bf16[3,4,128,128]{3,0,2,1:T(4,128)(2,1)S(1)} %copy.170), channel_id=1, source_target_pairs={{440,0},{448,8},{456,16},{464,24},{472,32},{480,40},{488,48},{496,... | collective-permute-start | bytes 1179656 | tf_op jit(solution)/shard_map/ppermute | solution.py:13
  758.7 19.6 %collective-permute-done.61 = bf16[3,4,128,128]{3,0,2,1:T(4,128)(2,1)S(1)} collective-permute-done((bf16[3,4,128,128]{3,0,2,1:T(4,128)(2,1)S(1)}, bf16[3,4,128,128]{3,0,2,1:T(4,128)(2,1)S(1)}, u32[]{:S(2)}, u32[]{:S(2)}) %collective-permute-start.61) | collective-permute-done | bytes 393248 | tf_op jit(solution)/shard_map/ppermute | solution.py:13
  778.3 76.2 %collective-permute-start.66 = (bf16[3,4,128,128]{3,0,2,1:T(4,128)(2,1)S(1)}, bf16[3,4,128,128]{3,0,2,1:T(4,128)(2,1)}, u32[]{:S(2)}, u32[]{:S(2)}) collective-permute-start(bf16[3,4,128,128]{3,0,2,1:T(4,128)(2,1)S(1)} %copy.170), channel_id=1, source_target_pairs={{448,0},{456,8},{464,16},{472,24},{480,32},{488,40},{496,48},{504,... | collective-permute-start | bytes 1179656 | tf_op jit(solution)/shard_map/ppermute | solution.py:13
  854.6 60.5 %collective-permute-start.67 = (bf16[3,4,128,128]{3,0,2,1:T(4,128)(2,1)S(1)}, bf16[3,4,128,128]{3,0,2,1:T(4,128)(2,1)}, u32[]{:S(2)}, u32[]{:S(2)}) collective-permute-start(bf16[3,4,128,128]{3,0,2,1:T(4,128)(2,1)S(1)} %copy.170), channel_id=1, source_target_pairs={{456,0},{464,8},{472,16},{480,24},{488,32},{496,40},{504,48},{0,56... | collective-permute-start | bytes 1179656 | tf_op jit(solution)/shard_map/ppermute | solution.py:13
  919.2 13.1 %collective-permute-done.66 = bf16[3,4,128,128]{3,0,2,1:T(4,128)(2,1)} collective-permute-done((bf16[3,4,128,128]{3,0,2,1:T(4,128)(2,1)S(1)}, bf16[3,4,128,128]{3,0,2,1:T(4,128)(2,1)}, u32[]{:S(2)}, u32[]{:S(2)}) %collective-permute-start.66) | collective-permute-done | bytes 393248 | tf_op jit(solution)/shard_map/ppermute | solution.py:13
  932.4 21.8 %collective-permute-done.67 = bf16[3,4,128,128]{3,0,2,1:T(4,128)(2,1)} collective-permute-done((bf16[3,4,128,128]{3,0,2,1:T(4,128)(2,1)S(1)}, bf16[3,4,128,128]{3,0,2,1:T(4,128)(2,1)}, u32[]{:S(2)}, u32[]{:S(2)}) %collective-permute-start.67) | collective-permute-done | bytes 393248 | tf_op jit(solution)/shard_map/ppermute | solution.py:13
  954.2 28.1 %collective-permute-done.68 = bf16[3,4,128,128]{3,0,2,1:T(4,128)(2,1)} collective-permute-done((bf16[3,4,128,128]{3,0,2,1:T(4,128)(2,1)S(1)}, bf16[3,4,128,128]{3,0,2,1:T(4,128)(2,1)}, u32[]{:S(2)}, u32[]{:S(2)}) %collective-permute-start.68) | collective-permute-done | bytes 393248 | tf_op jit(solution)/shard_map/ppermute | solution.py:13
  982.3 153.6 %concatenate.18 = bf16[72,4,128,128]{3,0,2,1:T(8,128)(2,1)} concatenate(bf16[3,4,128,128]{3,0,2,1:T(4,128)(2,1)S(1)} %copy.170, bf16[3,4,128,128]{3,0,2,1:T(4,128)(2,1)S(1)} %collective-permute-done.46, bf16[3,4,128,128]{3,0,2,1:T(4,128)(2,1)S(1)} %collective-permute-done.47, bf16[3,4,128,128]{3,0,2,1:T(4,128)(2,1)S(1)} %collective-permute-done.48, ...), dimensions={0} | concatenate | bytes 18874368 | tf_op jit(solution)/shard_map/concatenate | solution.py:46
  1135.8 78.9 %while.11 = (s32[]{:T(128)}, f32[3,4,128,128]{2,3,1,0:T(8,128)S(1)}, s32[4]{0:T(128)S(1)}, s32[3,32]{1,0:T(4,128)S(1)}, s32[72]{0:T(128)S(1)}, /*index=5*/pred[7...) while((s32[]{:T(128)}, ...), condition=%wide.region_3.4_spmd.clone, body=%wide.region_1.3_spmd.clone.sunk | while | flops 645681728 | bytes 24386944 | solution.py:84
  1137.2 6.8 fusion.48
  1144.5 7.7 fusion.49
  1156.9 6.8 fusion.48
  1164.2 7.7 fusion.49
  1176.6 6.8 fusion.48
  1183.9 7.7 fusion.49
  1196.3 6.8 fusion.48
  1203.6 7.7 fusion.49
  (214 shorter events, 127.5 us)
Async XLA Ops:
  6.5 1129.3 %all-gather.4.cloned.1.call-start = ((), (), s32[]{:S(2)}) async-start(), calls=%async_computation | async-start | bytes 3538944 | tf_op jit(solution)/shard_map/all_gather | solution.py:30
  7.3 27.2 %collective-permute-start = (s32[3,1]{0,1:T(1,128)}, s32[3,1]{0,1:T(1,128)S(1)}, u32[]{:S(2)}, u32[]{:S(2)}) collective-permute-start(s32[3,1]{0,1:T(1,128)} %param.7), channel_id=1, source_target_pairs={{8,0},{16,8},{24,16},{32,24},{40,32},{48,40},{56,48},{64,56},{72,6... | collective-permute-start | bytes 44 | tf_op jit(solution)/shard_map/ppermute | solution.py:13
  9.2 27.9 %collective-permute-start.1 = (s32[3,1]{0,1:T(1,128)}, s32[3,1]{0,1:T(1,128)S(1)}, u32[]{:S(2)}, u32[]{:S(2)}) collective-permute-start(s32[3,1]{0,1:T(1,128)} %param.7), channel_id=1, source_target_pairs={{56,0},{64,8},{72,16},{80,24},{88,32},{96,40},{104,48},{112,56},{1... | collective-permute-start | bytes 44 | tf_op jit(solution)/shard_map/ppermute | solution.py:13
  22.3 335.0 %collective-permute-start.46 = (bf16[3,4,128,128]{3,0,2,1:T(4,128)(2,1)S(1)}, bf16[3,4,128,128]{3,0,2,1:T(4,128)(2,1)S(1)}, u32[]{:S(2)}, u32[]{:S(2)}) collective-permute-start(bf16[3,4,128,128]{3,0,2,1:T(4,128)(2,1)S(1)} %copy.170), channel_id=1, source_target_pairs={{8,0},{16,8},{24,16},{32,24},{40,32},{48,40},{56,48},{64,56},{72,6... | collective-permute-start | bytes 1179656 | tf_op jit(solution)/shard_map/ppermute | solution.py:13
  24.8 340.8 %collective-permute-start.47 = (bf16[3,4,128,128]{3,0,2,1:T(4,128)(2,1)S(1)}, bf16[3,4,128,128]{3,0,2,1:T(4,128)(2,1)S(1)}, u32[]{:S(2)}, u32[]{:S(2)}) collective-permute-start(bf16[3,4,128,128]{3,0,2,1:T(4,128)(2,1)S(1)} %copy.170), channel_id=1, source_target_pairs={{56,0},{64,8},{72,16},{80,24},{88,32},{96,40},{104,48},{112,56},{1... | collective-permute-start | bytes 1179656 | tf_op jit(solution)/shard_map/ppermute | solution.py:13
  29.8 340.9 %collective-permute-start.48 = (bf16[3,4,128,128]{3,0,2,1:T(4,128)(2,1)S(1)}, bf16[3,4,128,128]{3,0,2,1:T(4,128)(2,1)S(1)}, u32[]{:S(2)}, u32[]{:S(2)}) collective-permute-start(bf16[3,4,128,128]{3,0,2,1:T(4,128)(2,1)S(1)} %copy.170), channel_id=1, source_target_pairs={{64,0},{72,8},{80,16},{88,24},{96,32},{104,40},{112,48},{120,56},{... | collective-permute-start | bytes 1179656 | tf_op jit(solution)/shard_map/ppermute | solution.py:13
  40.4 50.1 %collective-permute-start.12 = (s32[3,1]{0,1:T(1,128)}, s32[3,1]{0,1:T(1,128)S(1)}, u32[]{:S(2)}, u32[]{:S(2)}) collective-permute-start(s32[3,1]{0,1:T(1,128)} %param.7), channel_id=1, source_target_pairs={{264,0},{272,8},{280,16},{288,24},{296,32},{304,40},{312,48},{320,... | collective-permute-start | bytes 44 | tf_op jit(solution)/shard_map/ppermute | solution.py:13
  43.4 61.8 %collective-permute-start.13 = (s32[3,1]{0,1:T(1,128)}, s32[3,1]{0,1:T(1,128)S(1)}, u32[]{:S(2)}, u32[]{:S(2)}) collective-permute-start(s32[3,1]{0,1:T(1,128)} %param.7), channel_id=1, source_target_pairs={{312,0},{320,8},{328,16},{336,24},{344,32},{352,40},{360,48},{368,... | collective-permute-start | bytes 44 | tf_op jit(solution)/shard_map/ppermute | solution.py:13
  90.4 20.3 %collective-permute-start.14 = (s32[3,1]{0,1:T(1,128)}, s32[3,1]{0,1:T(1,128)S(1)}, u32[]{:S(2)}, u32[]{:S(2)}) collective-permute-start(s32[3,1]{0,1:T(1,128)} %param.7), channel_id=1, source_target_pairs={{320,0},{328,8},{336,16},{344,24},{352,32},{360,40},{368,48},{376,... | collective-permute-start | bytes 44 | tf_op jit(solution)/shard_map/ppermute | solution.py:13
  105.1 12.7 %collective-permute-start.15 = (s32[3,1]{0,1:T(1,128)}, s32[3,1]{0,1:T(1,128)S(1)}, u32[]{:S(2)}, u32[]{:S(2)}) collective-permute-start(s32[3,1]{0,1:T(1,128)} %param.7), channel_id=1, source_target_pairs={{328,0},{336,8},{344,16},{352,24},{360,32},{368,40},{376,48},{384,... | collective-permute-start | bytes 44 | tf_op jit(solution)/shard_map/ppermute | solution.py:13
  110.8 18.7 %collective-permute-start.16 = (s32[3,1]{0,1:T(1,128)}, s32[3,1]{0,1:T(1,128)S(1)}, u32[]{:S(2)}, u32[]{:S(2)}) collective-permute-start(s32[3,1]{0,1:T(1,128)} %param.7), channel_id=1, source_target_pairs={{376,0},{384,8},{392,16},{400,24},{408,32},{416,40},{424,48},{432,... | collective-permute-start | bytes 44 | tf_op jit(solution)/shard_map/ppermute | solution.py:13
  117.9 22.8 %collective-permute-start.17 = (s32[3,1]{0,1:T(1,128)}, s32[3,1]{0,1:T(1,128)S(1)}, u32[]{:S(2)}, u32[]{:S(2)}) collective-permute-start(s32[3,1]{0,1:T(1,128)} %param.7), channel_id=1, source_target_pairs={{384,0},{392,8},{400,16},{408,24},{416,32},{424,40},{432,48},{440,... | collective-permute-start | bytes 44 | tf_op jit(solution)/shard_map/ppermute | solution.py:13
  129.4 14.6 %collective-permute-start.18 = (s32[3,1]{0,1:T(1,128)}, s32[3,1]{0,1:T(1,128)S(1)}, u32[]{:S(2)}, u32[]{:S(2)}) collective-permute-start(s32[3,1]{0,1:T(1,128)} %param.7), channel_id=1, source_target_pairs={{392,0},{400,8},{408,16},{416,24},{424,32},{432,40},{440,48},{448,... | collective-permute-start | bytes 44 | tf_op jit(solution)/shard_map/ppermute | solution.py:13
  140.7 13.1 %collective-permute-start.19 = (s32[3,1]{0,1:T(1,128)}, s32[3,1]{0,1:T(1,128)S(1)}, u32[]{:S(2)}, u32[]{:S(2)}) collective-permute-start(s32[3,1]{0,1:T(1,128)} %param.7), channel_id=1, source_target_pairs={{440,0},{448,8},{456,16},{464,24},{472,32},{480,40},{488,48},{496,... | collective-permute-start | bytes 44 | tf_op jit(solution)/shard_map/ppermute | solution.py:13
  144.0 11.7 collective-permute-start.2
  153.9 10.7 collective-permute-start.20
  155.8 15.7 %collective-permute-start.21 = (s32[3,1]{0,1:T(1,128)}, s32[3,1]{0,1:T(1,128)S(1)}, u32[]{:S(2)}, u32[]{:S(2)}) collective-permute-start(s32[3,1]{0,1:T(1,128)} %param.7), channel_id=1, source_target_pairs={{456,0},{464,8},{472,16},{480,24},{488,32},{496,40},{504,48},{0,56... | collective-permute-start | bytes 44 | tf_op jit(solution)/shard_map/ppermute | solution.py:13
  164.6 11.8 collective-permute-start.22
  171.5 10.4 collective-permute-start.3
  176.5 14.3 %collective-permute-start.4 = (s32[3,1]{0,1:T(1,128)}, s32[3,1]{0,1:T(1,128)S(1)}, u32[]{:S(2)}, u32[]{:S(2)}) collective-permute-start(s32[3,1]{0,1:T(1,128)} %param.7), channel_id=1, source_target_pairs={{120,0},{128,8},{136,16},{144,24},{152,32},{160,40},{168,48},{176,... | collective-permute-start | bytes 44 | tf_op jit(solution)/shard_map/ppermute | solution.py:13
  182.0 16.8 %collective-permute-start.5 = (s32[3,1]{0,1:T(1,128)}, s32[3,1]{0,1:T(1,128)S(1)}, u32[]{:S(2)}, u32[]{:S(2)}) collective-permute-start(s32[3,1]{0,1:T(1,128)} %param.7), channel_id=1, source_target_pairs={{128,0},{136,8},{144,16},{152,24},{160,32},{168,40},{176,48},{184,... | collective-permute-start | bytes 44 | tf_op jit(solution)/shard_map/ppermute | solution.py:13
  190.7 13.7 %collective-permute-start.6 = (s32[3,1]{0,1:T(1,128)}, s32[3,1]{0,1:T(1,128)S(1)}, u32[]{:S(2)}, u32[]{:S(2)}) collective-permute-start(s32[3,1]{0,1:T(1,128)} %param.7), channel_id=1, source_target_pairs={{136,0},{144,8},{152,16},{160,24},{168,32},{176,40},{184,48},{192,... | collective-permute-start | bytes 44 | tf_op jit(solution)/shard_map/ppermute | solution.py:13
  198.8 11.6 collective-permute-start.7
  204.4 11.0 collective-permute-start.8
  210.4 9.6 collective-permute-start.9
  215.5 9.7 collective-permute-start.23
  220.0 11.0 collective-permute-start.24
  225.2 10.3 collective-permute-start.25
  230.9 13.3 %collective-permute-start.26 = (s32[3,4]{0,1:T(4,128)S(1)}, s32[3,4]{0,1:T(4,128)S(1)}, u32[]{:S(2)}, u32[]{:S(2)}) collective-permute-start(s32[3,4]{0,1:T(4,128)S(1)} %copy.146), channel_id=1, source_target_pairs={{72,0},{80,8},{88,16},{96,24},{104,32},{112,40},{120,48},{128,56},... | collective-permute-start | bytes 152 | tf_op jit(solution)/shard_map/ppermute | solution.py:13
  235.5 17.9 %collective-permute-start.27 = (s32[3,4]{0,1:T(4,128)S(1)}, s32[3,4]{0,1:T(4,128)S(1)}, u32[]{:S(2)}, u32[]{:S(2)}) collective-permute-start(s32[3,4]{0,1:T(4,128)S(1)} %copy.146), channel_id=1, source_target_pairs={{120,0},{128,8},{136,16},{144,24},{152,32},{160,40},{168,48},{176,... | collective-permute-start | bytes 152 | tf_op jit(solution)/shard_map/ppermute | solution.py:13
  244.3 14.9 %collective-permute-start.28 = (s32[3,4]{0,1:T(4,128)S(1)}, s32[3,4]{0,1:T(4,128)S(1)}, u32[]{:S(2)}, u32[]{:S(2)}) collective-permute-start(s32[3,4]{0,1:T(4,128)S(1)} %copy.146), channel_id=1, source_target_pairs={{128,0},{136,8},{144,16},{152,24},{160,32},{168,40},{176,48},{184,... | collective-permute-start | bytes 152 | tf_op jit(solution)/shard_map/ppermute | solution.py:13
  253.4 13.6 %collective-permute-start.29 = (s32[3,4]{0,1:T(4,128)S(1)}, s32[3,4]{0,1:T(4,128)S(1)}, u32[]{:S(2)}, u32[]{:S(2)}) collective-permute-start(s32[3,4]{0,1:T(4,128)S(1)} %copy.146), channel_id=1, source_target_pairs={{136,0},{144,8},{152,16},{160,24},{168,32},{176,40},{184,48},{192,... | collective-permute-start | bytes 152 | tf_op jit(solution)/shard_map/ppermute | solution.py:13
  259.1 12.0 collective-permute-start.30
  267.0 9.4 collective-permute-start.31
  282.6 9.5 collective-permute-start.35
  285.4 11.9 collective-permute-start.36
  292.2 10.3 collective-permute-start.37
  297.4 12.5 %collective-permute-start.38 = (s32[3,4]{0,1:T(4,128)S(1)}, s32[3,4]{0,1:T(4,128)S(1)}, u32[]{:S(2)}, u32[]{:S(2)}) collective-permute-start(s32[3,4]{0,1:T(4,128)S(1)} %copy.146), channel_id=1, source_target_pairs={{328,0},{336,8},{344,16},{352,24},{360,32},{368,40},{376,48},{384,... | collective-permute-start | bytes 152 | tf_op jit(solution)/shard_map/ppermute | solution.py:13
  302.4 14.7 %collective-permute-start.39 = (s32[3,4]{0,1:T(4,128)S(1)}, s32[3,4]{0,1:T(4,128)S(1)}, u32[]{:S(2)}, u32[]{:S(2)}) collective-permute-start(s32[3,4]{0,1:T(4,128)S(1)} %copy.146), channel_id=1, source_target_pairs={{376,0},{384,8},{392,16},{400,24},{408,32},{416,40},{424,48},{432,... | collective-permute-start | bytes 152 | tf_op jit(solution)/shard_map/ppermute | solution.py:13
  309.9 15.1 %collective-permute-start.40 = (s32[3,4]{0,1:T(4,128)S(1)}, s32[3,4]{0,1:T(4,128)S(1)}, u32[]{:S(2)}, u32[]{:S(2)}) collective-permute-start(s32[3,4]{0,1:T(4,128)S(1)} %copy.146), channel_id=1, source_target_pairs={{384,0},{392,8},{400,16},{408,24},{416,32},{424,40},{432,48},{440,... | collective-permute-start | bytes 152 | tf_op jit(solution)/shard_map/ppermute | solution.py:13
  317.1 14.5 %collective-permute-start.41 = (s32[3,4]{0,1:T(4,128)S(1)}, s32[3,4]{0,1:T(4,128)S(1)}, u32[]{:S(2)}, u32[]{:S(2)}) collective-permute-start(s32[3,4]{0,1:T(4,128)S(1)} %copy.146), channel_id=1, source_target_pairs={{392,0},{400,8},{408,16},{416,24},{424,32},{432,40},{440,48},{448,... | collective-permute-start | bytes 152 | tf_op jit(solution)/shard_map/ppermute | solution.py:13
  325.0 11.9 collective-permute-start.42
  331.7 10.3 collective-permute-start.43
  336.9 9.7 collective-permute-start.44
  346.6 59.5 %collective-permute-start.49 = (bf16[3,4,128,128]{3,0,2,1:T(4,128)(2,1)S(1)}, bf16[3,4,128,128]{3,0,2,1:T(4,128)(2,1)S(1)}, u32[]{:S(2)}, u32[]{:S(2)}) collective-permute-start(bf16[3,4,128,128]{3,0,2,1:T(4,128)(2,1)S(1)} %copy.170), channel_id=1, source_target_pairs={{72,0},{80,8},{88,16},{96,24},{104,32},{112,40},{120,48},{128,56},... | collective-permute-start | bytes 1179656 | tf_op jit(solution)/shard_map/ppermute | solution.py:13
  348.6 107.7 %collective-permute-start.50 = (bf16[3,4,128,128]{3,0,2,1:T(4,128)(2,1)S(1)}, bf16[3,4,128,128]{3,0,2,1:T(4,128)(2,1)S(1)}, u32[]{:S(2)}, u32[]{:S(2)}) collective-permute-start(bf16[3,4,128,128]{3,0,2,1:T(4,128)(2,1)S(1)} %copy.170), channel_id=1, source_target_pairs={{120,0},{128,8},{136,16},{144,24},{152,32},{160,40},{168,48},{176,... | collective-permute-start | bytes 1179656 | tf_op jit(solution)/shard_map/ppermute | solution.py:13
  357.3 121.4 %collective-permute-start.51 = (bf16[3,4,128,128]{3,0,2,1:T(4,128)(2,1)S(1)}, bf16[3,4,128,128]{3,0,2,1:T(4,128)(2,1)S(1)}, u32[]{:S(2)}, u32[]{:S(2)}) collective-permute-start(bf16[3,4,128,128]{3,0,2,1:T(4,128)(2,1)S(1)} %copy.170), channel_id=1, source_target_pairs={{128,0},{136,8},{144,16},{152,24},{160,32},{168,40},{176,48},{184,... | collective-permute-start | bytes 1179656 | tf_op jit(solution)/shard_map/ppermute | solution.py:13
  365.6 144.4 %collective-permute-start.52 = (bf16[3,4,128,128]{3,0,2,1:T(4,128)(2,1)S(1)}, bf16[3,4,128,128]{3,0,2,1:T(4,128)(2,1)S(1)}, u32[]{:S(2)}, u32[]{:S(2)}) collective-permute-start(bf16[3,4,128,128]{3,0,2,1:T(4,128)(2,1)S(1)} %copy.170), channel_id=1, source_target_pairs={{136,0},{144,8},{152,16},{160,24},{168,32},{176,40},{184,48},{192,... | collective-permute-start | bytes 1179656 | tf_op jit(solution)/shard_map/ppermute | solution.py:13
  370.7 179.7 %collective-permute-start.53 = (bf16[3,4,128,128]{3,0,2,1:T(4,128)(2,1)S(1)}, bf16[3,4,128,128]{3,0,2,1:T(4,128)(2,1)S(1)}, u32[]{:S(2)}, u32[]{:S(2)}) collective-permute-start(bf16[3,4,128,128]{3,0,2,1:T(4,128)(2,1)S(1)} %copy.170), channel_id=1, source_target_pairs={{184,0},{192,8},{200,16},{208,24},{216,32},{224,40},{232,48},{240,... | collective-permute-start | bytes 1179656 | tf_op jit(solution)/shard_map/ppermute | solution.py:13
  406.1 248.9 %collective-permute-start.54 = (bf16[3,4,128,128]{3,0,2,1:T(4,128)(2,1)S(1)}, bf16[3,4,128,128]{3,0,2,1:T(4,128)(2,1)}, u32[]{:S(2)}, u32[]{:S(2)}) collective-permute-start(bf16[3,4,128,128]{3,0,2,1:T(4,128)(2,1)S(1)} %copy.170), channel_id=1, source_target_pairs={{192,0},{200,8},{208,16},{216,24},{224,32},{232,40},{240,48},{248,... | collective-permute-start | bytes 1179656 | tf_op jit(solution)/shard_map/ppermute | solution.py:13
  456.2 200.8 %collective-permute-start.55 = (bf16[3,4,128,128]{3,0,2,1:T(4,128)(2,1)S(1)}, bf16[3,4,128,128]{3,0,2,1:T(4,128)(2,1)}, u32[]{:S(2)}, u32[]{:S(2)}) collective-permute-start(bf16[3,4,128,128]{3,0,2,1:T(4,128)(2,1)S(1)} %copy.170), channel_id=1, source_target_pairs={{200,0},{208,8},{216,16},{224,24},{232,32},{240,40},{248,48},{256,... | collective-permute-start | bytes 1179656 | tf_op jit(solution)/shard_map/ppermute | solution.py:13
  478.7 185.1 %collective-permute-start.56 = (bf16[3,4,128,128]{3,0,2,1:T(4,128)(2,1)S(1)}, bf16[3,4,128,128]{3,0,2,1:T(4,128)(2,1)}, u32[]{:S(2)}, u32[]{:S(2)}) collective-permute-start(bf16[3,4,128,128]{3,0,2,1:T(4,128)(2,1)S(1)} %copy.170), channel_id=1, source_target_pairs={{248,0},{256,8},{264,16},{272,24},{280,32},{288,40},{296,48},{304,... | collective-permute-start | bytes 1179656 | tf_op jit(solution)/shard_map/ppermute | solution.py:13
  510.1 173.4 %collective-permute-start.57 = (bf16[3,4,128,128]{3,0,2,1:T(4,128)(2,1)S(1)}, bf16[3,4,128,128]{3,0,2,1:T(4,128)(2,1)}, u32[]{:S(2)}, u32[]{:S(2)}) collective-permute-start(bf16[3,4,128,128]{3,0,2,1:T(4,128)(2,1)S(1)} %copy.170), channel_id=1, source_target_pairs={{256,0},{264,8},{272,16},{280,24},{288,32},{296,40},{304,48},{312,... | collective-permute-start | bytes 1179656 | tf_op jit(solution)/shard_map/ppermute | solution.py:13
  550.5 135.0 %collective-permute-start.58 = (bf16[3,4,128,128]{3,0,2,1:T(4,128)(2,1)S(1)}, bf16[3,4,128,128]{3,0,2,1:T(4,128)(2,1)}, u32[]{:S(2)}, u32[]{:S(2)}) collective-permute-start(bf16[3,4,128,128]{3,0,2,1:T(4,128)(2,1)S(1)} %copy.170), channel_id=1, source_target_pairs={{264,0},{272,8},{280,16},{288,24},{296,32},{304,40},{312,48},{320,... | collective-permute-start | bytes 1179656 | tf_op jit(solution)/shard_map/ppermute | solution.py:13
  655.1 75.0 %collective-permute-start.59 = (bf16[3,4,128,128]{3,0,2,1:T(4,128)(2,1)S(1)}, bf16[3,4,128,128]{3,0,2,1:T(4,128)(2,1)S(1)}, u32[]{:S(2)}, u32[]{:S(2)}) collective-permute-start(bf16[3,4,128,128]{3,0,2,1:T(4,128)(2,1)S(1)} %copy.170), channel_id=1, source_target_pairs={{312,0},{320,8},{328,16},{336,24},{344,32},{352,40},{360,48},{368,... | collective-permute-start | bytes 1179656 | tf_op jit(solution)/shard_map/ppermute | solution.py:13
  657.0 84.9 %collective-permute-start.60 = (bf16[3,4,128,128]{3,0,2,1:T(4,128)(2,1)S(1)}, bf16[3,4,128,128]{3,0,2,1:T(4,128)(2,1)S(1)}, u32[]{:S(2)}, u32[]{:S(2)}) collective-permute-start(bf16[3,4,128,128]{3,0,2,1:T(4,128)(2,1)S(1)} %copy.170), channel_id=1, source_target_pairs={{320,0},{328,8},{336,16},{344,24},{352,32},{360,40},{368,48},{376,... | collective-permute-start | bytes 1179656 | tf_op jit(solution)/shard_map/ppermute | solution.py:13
  663.8 114.5 %collective-permute-start.61 = (bf16[3,4,128,128]{3,0,2,1:T(4,128)(2,1)S(1)}, bf16[3,4,128,128]{3,0,2,1:T(4,128)(2,1)S(1)}, u32[]{:S(2)}, u32[]{:S(2)}) collective-permute-start(bf16[3,4,128,128]{3,0,2,1:T(4,128)(2,1)S(1)} %copy.170), channel_id=1, source_target_pairs={{328,0},{336,8},{344,16},{352,24},{360,32},{368,40},{376,48},{384,... | collective-permute-start | bytes 1179656 | tf_op jit(solution)/shard_map/ppermute | solution.py:13
  683.5 171.0 %collective-permute-start.62 = (bf16[3,4,128,128]{3,0,2,1:T(4,128)(2,1)S(1)}, bf16[3,4,128,128]{3,0,2,1:T(4,128)(2,1)S(1)}, u32[]{:S(2)}, u32[]{:S(2)}) collective-permute-start(bf16[3,4,128,128]{3,0,2,1:T(4,128)(2,1)S(1)} %copy.170), channel_id=1, source_target_pairs={{376,0},{384,8},{392,16},{400,24},{408,32},{416,40},{424,48},{432,... | collective-permute-start | bytes 1179656 | tf_op jit(solution)/shard_map/ppermute | solution.py:13
  685.4 229.6 %collective-permute-start.63 = (bf16[3,4,128,128]{3,0,2,1:T(4,128)(2,1)S(1)}, bf16[3,4,128,128]{3,0,2,1:T(4,128)(2,1)S(1)}, u32[]{:S(2)}, u32[]{:S(2)}) collective-permute-start(bf16[3,4,128,128]{3,0,2,1:T(4,128)(2,1)S(1)} %copy.170), channel_id=1, source_target_pairs={{384,0},{392,8},{400,16},{408,24},{416,32},{424,40},{432,48},{440,... | collective-permute-start | bytes 1179656 | tf_op jit(solution)/shard_map/ppermute | solution.py:13
  730.1 189.1 %collective-permute-start.64 = (bf16[3,4,128,128]{3,0,2,1:T(4,128)(2,1)S(1)}, bf16[3,4,128,128]{3,0,2,1:T(4,128)(2,1)}, u32[]{:S(2)}, u32[]{:S(2)}) collective-permute-start(bf16[3,4,128,128]{3,0,2,1:T(4,128)(2,1)S(1)} %copy.170), channel_id=1, source_target_pairs={{392,0},{400,8},{408,16},{416,24},{424,32},{432,40},{440,48},{448,... | collective-permute-start | bytes 1179656 | tf_op jit(solution)/shard_map/ppermute | solution.py:13
  741.9 177.3 %collective-permute-start.65 = (bf16[3,4,128,128]{3,0,2,1:T(4,128)(2,1)S(1)}, bf16[3,4,128,128]{3,0,2,1:T(4,128)(2,1)}, u32[]{:S(2)}, u32[]{:S(2)}) collective-permute-start(bf16[3,4,128,128]{3,0,2,1:T(4,128)(2,1)S(1)} %copy.170), channel_id=1, source_target_pairs={{440,0},{448,8},{456,16},{464,24},{472,32},{480,40},{488,48},{496,... | collective-permute-start | bytes 1179656 | tf_op jit(solution)/shard_map/ppermute | solution.py:13
  778.3 154.0 %collective-permute-start.66 = (bf16[3,4,128,128]{3,0,2,1:T(4,128)(2,1)S(1)}, bf16[3,4,128,128]{3,0,2,1:T(4,128)(2,1)}, u32[]{:S(2)}, u32[]{:S(2)}) collective-permute-start(bf16[3,4,128,128]{3,0,2,1:T(4,128)(2,1)S(1)} %copy.170), channel_id=1, source_target_pairs={{448,0},{456,8},{464,16},{472,24},{480,32},{488,40},{496,48},{504,... | collective-permute-start | bytes 1179656 | tf_op jit(solution)/shard_map/ppermute | solution.py:13
  854.6 99.6 %collective-permute-start.67 = (bf16[3,4,128,128]{3,0,2,1:T(4,128)(2,1)S(1)}, bf16[3,4,128,128]{3,0,2,1:T(4,128)(2,1)}, u32[]{:S(2)}, u32[]{:S(2)}) collective-permute-start(bf16[3,4,128,128]{3,0,2,1:T(4,128)(2,1)S(1)} %copy.170), channel_id=1, source_target_pairs={{456,0},{464,8},{472,16},{480,24},{488,32},{496,40},{504,48},{0,56... | collective-permute-start | bytes 1179656 | tf_op jit(solution)/shard_map/ppermute | solution.py:13
  915.0 67.2 %collective-permute-start.68 = (bf16[3,4,128,128]{3,0,2,1:T(4,128)(2,1)S(1)}, bf16[3,4,128,128]{3,0,2,1:T(4,128)(2,1)}, u32[]{:S(2)}, u32[]{:S(2)}) collective-permute-start(bf16[3,4,128,128]{3,0,2,1:T(4,128)(2,1)S(1)} %copy.170), channel_id=1, source_target_pairs={{504,0},{0,8},{8,16},{16,24},{24,32},{32,40},{40,48},{48,56},{56,6... | collective-permute-start | bytes 1179656 | tf_op jit(solution)/shard_map/ppermute | solution.py:13
  (39 other events, 4939.8 us)
Sparse Core Ops, SparseCore 0:
  10.6 79.5 all-gather.3
where the time goes:
time: 1230 us; the launch traced here: 1220 us
  starting transfers between devices  563 us (46%)
  waiting for transfers between devices  352 us (29%)
  local copies, waits for them, and re-layouts  162 us (13%)
  matrix products  71.5 us (6%)
  blocking collectives  49.1 us (4%)
  between operations  15 us (1%)
    ppermute x69, starting transfers between devices, from_behind(): return lax.ppermute(block, axis, route)  563 us
    ppermute x69, waiting for transfers between devices, from_behind(): return lax.ppermute(block, axis, route)  351 us
    concatenate x1, local copies, waits for them, and re-layouts, body(): stack_tiles = jnp.concatenate([piece[0] for piece in pieces], axis=0)  154 us
    all_gather x1, blocking collectives, body(): lax.all_gather(tile_cols, 'col', axis=1, tiled=True)  30.9 us
    dot_general x4, matrix products, advance(): jnp.einsum('rgus,rguxy->rgsxy', hits, chosen, preferred_element_type=jnp....  30.8 us
    dot_general x4, matrix products, advance(): jnp.einsum('rgf,fuxy->rguxy', matches.astype(jnp.bfloat16), stack_tiles,...  27.2 us
  transfers between devices with their start and end apart: 70, of which 26 were waited for; matrix products, arithmetic and copies ran while one was open for 13% of the time, Pallas kernels for 0%

commit v1 on v0

--- a/solution.py
+++ b/solution.py
@@ -28,7 +28,9 @@
     own_live = slot_live(tile_cols, tile_counts)
     left_tiles, left_cols, left_counts = (
         lax.all_gather(x_tiles, "col", axis=1, tiled=True),
-        lax.all_gather(tile_cols, "col", axis=1, tiled=True),
+        jnp.concatenate(
+            lax.all_to_all(jnp.stack([tile_cols] * lax.axis_size("col")), "col", 0, 0), axis=1
+        ),
         lax.all_gather(tile_counts, "col", axis=1, tiled=True),
     )
     left_keyed = jnp.where(slot_live(left_cols, left_counts), left_cols, -1).astype(jnp.int32)

time: 1230 us -> 1200 us (0.976)
  the two profiles are of different devices: /device:TPU:80 before, /device:TPU:4 now
where the time goes in v1:
time: 1200 us; the launch traced here: 1190 us
  starting transfers between devices  505 us (42%)
  waiting for transfers between devices  401 us (33%)
  local copies, waits for them, and re-layouts  162 us (14%)
  matrix products  71.5 us (6%)
  blocking collectives  15.8 us (1%)
  between operations  14.6 us (1%)
    ppermute x69, starting transfers between devices, from_behind(): return lax.ppermute(block, axis, route)  498 us
    ppermute x69, waiting for transfers between devices, from_behind(): return lax.ppermute(block, axis, route)  400 us
    concatenate x1, local copies, waits for them, and re-layouts, body(): stack_tiles = jnp.concatenate([piece[0] for piece in pieces], axis=0)  153 us
    dot_general x4, matrix products, advance(): jnp.einsum('rgus,rguxy->rgsxy', hits, chosen, preferred_element_type=jnp....  30.8 us
    dot_general x4, matrix products, advance(): jnp.einsum('rgf,fuxy->rguxy', matches.astype(jnp.bfloat16), stack_tiles,...  27.1 us
  transfers between devices with their start and end apart: 71, of which 31 were waited for; matrix products, arithmetic and copies ran while one was open for 14% of the time, Pallas kernels for 0%

profile of v1, /device:TPU:4, one launch (start us, length us, event | category | flops | bytes accessed | tf_op | source)
XLA Modules:
  0.0 1185.4 jit_solution(4918011812133014722)
XLA Ops:
  7.3 11.9 %collective-permute-start = (s32[3,1]{0,1:T(1,128)}, s32[3,1]{0,1:T(1,128)S(1)}, u32[]{:S(2)}, u32[]{:S(2)}) collective-permute-start(s32[3,1]{0,1:T(1,128)} %param.7), channel_id=1, source_target_pairs={{8,0},{16,8},{24,16},{32,24},{40,32},{48,40},{56,48},{64,56},{72,6... | collective-permute-start | bytes 44 | tf_op jit(solution)/shard_map/ppermute | solution.py:13
  35.2 7.1 all-to-all-start
  54.2 5.3 collective-permute-start.13
  59.5 59.7 %collective-permute-done.12 = s32[3,1]{0,1:T(1,128)S(1)} collective-permute-done((s32[3,1]{0,1:T(1,128)}, s32[3,1]{0,1:T(1,128)S(1)}, u32[]{:S(2)}, u32[]{:S(2)}) %collective-permute-start.12) | collective-permute-done | bytes 44 | tf_op jit(solution)/shard_map/ppermute | solution.py:13
  122.1 5.3 collective-permute-start.15
  129.6 7.3 collective-permute-start.16
  142.1 9.2 collective-permute-start.18
  156.7 6.4 collective-permute-start.2
  164.0 4.4 collective-permute-start.20
  182.5 6.2 collective-permute-start.4
  188.8 9.0 collective-permute-start.5
  197.8 5.8 collective-permute-start.6
  203.6 6.0 collective-permute-start.7
  211.5 5.5 collective-permute-start.8
  221.0 4.8 collective-permute-start.23
  229.0 5.5 collective-permute-start.25
  234.5 5.8 collective-permute-start.26
  240.4 6.0 collective-permute-start.27
  246.4 8.0 collective-permute-start.28
  254.5 7.2 collective-permute-start.29
  261.7 4.8 collective-permute-start.30
  268.1 5.1 collective-permute-start.31
  287.5 6.3 collective-permute-start.36
  293.8 5.4 collective-permute-start.37
  299.2 6.4 collective-permute-start.38
  305.6 5.9 collective-permute-start.39
  311.5 7.7 collective-permute-start.40
  319.2 6.8 collective-permute-start.41
  333.7 4.9 collective-permute-start.43
  352.5 6.4 collective-permute-start.50
  358.9 8.9 collective-permute-start.51
  367.8 4.6 collective-permute-start.52
  372.5 6.0 collective-permute-start.53
  380.7 28.6 %collective-permute-done.49 = bf16[3,4,128,128]{3,0,2,1:T(4,128)(2,1)S(1)} collective-permute-done((bf16[3,4,128,128]{3,0,2,1:T(4,128)(2,1)S(1)}, bf16[3,4,128,128]{3,0,2,1:T(4,128)(2,1)S(1)}, u32[]{:S(2)}, u32[]{:S(2)}) %collective-permute-start.49) | collective-permute-done | bytes 393248 | tf_op jit(solution)/shard_map/ppermute | solution.py:13
  409.3 5.1 collective-permute-start.54
  414.4 55.7 %collective-permute-done.50 = bf16[3,4,128,128]{3,0,2,1:T(4,128)(2,1)S(1)} collective-permute-done((bf16[3,4,128,128]{3,0,2,1:T(4,128)(2,1)S(1)}, bf16[3,4,128,128]{3,0,2,1:T(4,128)(2,1)S(1)}, u32[]{:S(2)}, u32[]{:S(2)}) %collective-permute-start.50) | collective-permute-done | bytes 393248 | tf_op jit(solution)/shard_map/ppermute | solution.py:13
  474.0 13.5 %collective-permute-done.52 = bf16[3,4,128,128]{3,0,2,1:T(4,128)(2,1)S(1)} collective-permute-done((bf16[3,4,128,128]{3,0,2,1:T(4,128)(2,1)S(1)}, bf16[3,4,128,128]{3,0,2,1:T(4,128)(2,1)S(1)}, u32[]{:S(2)}, u32[]{:S(2)}) %collective-permute-start.52) | collective-permute-done | bytes 393248 | tf_op jit(solution)/shard_map/ppermute | solution.py:13
  490.8 39.0 %collective-permute-done.53 = bf16[3,4,128,128]{3,0,2,1:T(4,128)(2,1)S(1)} collective-permute-done((bf16[3,4,128,128]{3,0,2,1:T(4,128)(2,1)S(1)}, bf16[3,4,128,128]{3,0,2,1:T(4,128)(2,1)S(1)}, u32[]{:S(2)}, u32[]{:S(2)}) %collective-permute-start.53) | collective-permute-done | bytes 393248 | tf_op jit(solution)/shard_map/ppermute | solution.py:13
  529.8 58.1 %collective-permute-start.58 = (bf16[3,4,128,128]{3,0,2,1:T(4,128)(2,1)S(1)}, bf16[3,4,128,128]{3,0,2,1:T(4,128)(2,1)}, u32[]{:S(2)}, u32[]{:S(2)}) collective-permute-start(bf16[3,4,128,128]{3,0,2,1:T(4,128)(2,1)S(1)} %copy.164), channel_id=1, source_target_pairs={{264,0},{272,8},{280,16},{288,24},{296,32},{304,40},{312,48},{320,... | collective-permute-start | bytes 1179656 | tf_op jit(solution)/shard_map/ppermute | solution.py:13
  588.7 15.8 %all-gather = s32[8,1,3]{2,1,0:T(1,128)S(1)} all-gather(s32[1,1,3]{2,1,0:T(1,128)} %bitcast.49), channel_id=1, replica_groups=mesh['row'=64,'col'=8] {'col'}, dimensions={0}, use_global_device_ids=true | all-gather | bytes 108 | tf_op jit(solution)/shard_map/all_gather | solution.py:34
  607.8 13.1 %collective-permute-done.55 = bf16[3,4,128,128]{3,0,2,1:T(4,128)(2,1)} collective-permute-done((bf16[3,4,128,128]{3,0,2,1:T(4,128)(2,1)S(1)}, bf16[3,4,128,128]{3,0,2,1:T(4,128)(2,1)}, u32[]{:S(2)}, u32[]{:S(2)}) %collective-permute-start.55) | collective-permute-done | bytes 393248 | tf_op jit(solution)/shard_map/ppermute | solution.py:13
  620.9 10.1 collective-permute-start.60
  634.1 7.0 collective-permute-start.61
  641.1 7.6 collective-permute-start.62
  648.8 10.4 collective-permute-start.63
  665.4 67.7 %collective-permute-done.60 = bf16[3,4,128,128]{3,0,2,1:T(4,128)(2,1)} collective-permute-done((bf16[3,4,128,128]{3,0,2,1:T(4,128)(2,1)S(1)}, bf16[3,4,128,128]{3,0,2,1:T(4,128)(2,1)}, u32[]{:S(2)}, u32[]{:S(2)}) %collective-permute-start.60) | collective-permute-done | bytes 393248 | tf_op jit(solution)/shard_map/ppermute | solution.py:13
  733.2 71.2 %collective-permute-start.65 = (bf16[3,4,128,128]{3,0,2,1:T(4,128)(2,1)S(1)}, bf16[3,4,128,128]{3,0,2,1:T(4,128)(2,1)}, u32[]{:S(2)}, u32[]{:S(2)}) collective-permute-start(bf16[3,4,128,128]{3,0,2,1:T(4,128)(2,1)S(1)} %copy.164), channel_id=1, source_target_pairs={{440,0},{448,8},{456,16},{464,24},{472,32},{480,40},{488,48},{496,... | collective-permute-start | bytes 1179656 | tf_op jit(solution)/shard_map/ppermute | solution.py:13
  804.3 7.8 collective-permute-done.61
  812.2 4.3 collective-permute-start.66
  816.4 16.9 %collective-permute-start.67 = (bf16[3,4,128,128]{3,0,2,1:T(4,128)(2,1)S(1)}, bf16[3,4,128,128]{3,0,2,1:T(4,128)(2,1)}, u32[]{:S(2)}, u32[]{:S(2)}) collective-permute-start(bf16[3,4,128,128]{3,0,2,1:T(4,128)(2,1)S(1)} %copy.164), channel_id=1, source_target_pairs={{456,0},{464,8},{472,16},{480,24},{488,32},{496,40},{504,48},{0,56... | collective-permute-start | bytes 1179656 | tf_op jit(solution)/shard_map/ppermute | solution.py:13
  833.3 28.1 %collective-permute-start.68 = (bf16[3,4,128,128]{3,0,2,1:T(4,128)(2,1)S(1)}, bf16[3,4,128,128]{3,0,2,1:T(4,128)(2,1)}, u32[]{:S(2)}, u32[]{:S(2)}) collective-permute-start(bf16[3,4,128,128]{3,0,2,1:T(4,128)(2,1)S(1)} %copy.164), channel_id=1, source_target_pairs={{504,0},{0,8},{8,16},{16,24},{24,32},{32,40},{40,48},{48,56},{56,6... | collective-permute-start | bytes 1179656 | tf_op jit(solution)/shard_map/ppermute | solution.py:13
  862.9 54.3 %collective-permute-done.66 = bf16[3,4,128,128]{3,0,2,1:T(4,128)(2,1)} collective-permute-done((bf16[3,4,128,128]{3,0,2,1:T(4,128)(2,1)S(1)}, bf16[3,4,128,128]{3,0,2,1:T(4,128)(2,1)}, u32[]{:S(2)}, u32[]{:S(2)}) %collective-permute-start.66) | collective-permute-done | bytes 393248 | tf_op jit(solution)/shard_map/ppermute | solution.py:13
  917.2 10.6 collective-permute-done.67
  927.8 17.6 %collective-permute-done.68 = bf16[3,4,128,128]{3,0,2,1:T(4,128)(2,1)} collective-permute-done((bf16[3,4,128,128]{3,0,2,1:T(4,128)(2,1)S(1)}, bf16[3,4,128,128]{3,0,2,1:T(4,128)(2,1)}, u32[]{:S(2)}, u32[]{:S(2)}) %collective-permute-start.68) | collective-permute-done | bytes 393248 | tf_op jit(solution)/shard_map/ppermute | solution.py:13
  945.4 153.3 %concatenate.18 = bf16[72,4,128,128]{3,0,2,1:T(8,128)(2,1)} concatenate(bf16[3,4,128,128]{3,0,2,1:T(4,128)(2,1)S(1)} %copy.164, bf16[3,4,128,128]{3,0,2,1:T(4,128)(2,1)S(1)} %collective-permute-done.46, bf16[3,4,128,128]{3,0,2,1:T(4,128)(2,1)S(1)} %collective-permute-done.47, bf16[3,4,128,128]{3,0,2,1:T(4,128)(2,1)S(1)} %collective-permute-done.48, ...), dimensions={0} | concatenate | bytes 18874368 | tf_op jit(solution)/shard_map/concatenate | solution.py:48
  1098.8 78.7 %while.11 = (s32[]{:T(128)}, f32[3,4,128,128]{2,3,1,0:T(8,128)S(1)}, s32[4]{0:T(128)S(1)}, s32[3,32]{1,0:T(4,128)S(1)}, s32[72]{0:T(128)S(1)}, /*index=5*/pred[7...) while((s32[]{:T(128)}, ...), condition=%wide.region_3.4_spmd.clone, body=%wide.region_1.3_spmd.clone.sunk | while | flops 645681728 | bytes 24386944 | solution.py:86
  1100.1 6.8 fusion.49
  1107.3 7.7 fusion.50
  1119.8 6.8 fusion.49
  1127.0 7.7 fusion.50
  1139.4 6.8 fusion.49
  1146.7 7.7 fusion.50
  1159.1 6.8 fusion.49
  1166.3 7.7 fusion.50
  (208 shorter events, 148.6 us)
Async XLA Ops:
  6.5 1092.2 %all-gather.3.cloned.1.call-start = ((), (), s32[]{:S(2)}) async-start(), calls=%async_computation.1 | async-start | bytes 3538944 | tf_op jit(solution)/shard_map/all_gather | solution.py:30
  7.3 38.1 %collective-permute-start = (s32[3,1]{0,1:T(1,128)}, s32[3,1]{0,1:T(1,128)S(1)}, u32[]{:S(2)}, u32[]{:S(2)}) collective-permute-start(s32[3,1]{0,1:T(1,128)} %param.7), channel_id=1, source_target_pairs={{8,0},{16,8},{24,16},{32,24},{40,32},{48,40},{56,48},{64,56},{72,6... | collective-permute-start | bytes 44 | tf_op jit(solution)/shard_map/ppermute | solution.py:13
  19.1 28.2 %collective-permute-start.1 = (s32[3,1]{0,1:T(1,128)}, s32[3,1]{0,1:T(1,128)S(1)}, u32[]{:S(2)}, u32[]{:S(2)}) collective-permute-start(s32[3,1]{0,1:T(1,128)} %param.7), channel_id=1, source_target_pairs={{56,0},{64,8},{72,16},{80,24},{88,32},{96,40},{104,48},{112,56},{1... | collective-permute-start | bytes 44 | tf_op jit(solution)/shard_map/ppermute | solution.py:13
  24.4 334.5 %collective-permute-start.46 = (bf16[3,4,128,128]{3,0,2,1:T(4,128)(2,1)S(1)}, bf16[3,4,128,128]{3,0,2,1:T(4,128)(2,1)S(1)}, u32[]{:S(2)}, u32[]{:S(2)}) collective-permute-start(bf16[3,4,128,128]{3,0,2,1:T(4,128)(2,1)S(1)} %copy.164), channel_id=1, source_target_pairs={{8,0},{16,8},{24,16},{32,24},{40,32},{48,40},{56,48},{64,56},{72,6... | collective-permute-start | bytes 1179656 | tf_op jit(solution)/shard_map/ppermute | solution.py:13
  28.1 339.7 %collective-permute-start.47 = (bf16[3,4,128,128]{3,0,2,1:T(4,128)(2,1)S(1)}, bf16[3,4,128,128]{3,0,2,1:T(4,128)(2,1)S(1)}, u32[]{:S(2)}, u32[]{:S(2)}) collective-permute-start(bf16[3,4,128,128]{3,0,2,1:T(4,128)(2,1)S(1)} %copy.164), channel_id=1, source_target_pairs={{56,0},{64,8},{72,16},{80,24},{88,32},{96,40},{104,48},{112,56},{1... | collective-permute-start | bytes 1179656 | tf_op jit(solution)/shard_map/ppermute | solution.py:13
  31.9 340.6 %collective-permute-start.48 = (bf16[3,4,128,128]{3,0,2,1:T(4,128)(2,1)S(1)}, bf16[3,4,128,128]{3,0,2,1:T(4,128)(2,1)S(1)}, u32[]{:S(2)}, u32[]{:S(2)}) collective-permute-start(bf16[3,4,128,128]{3,0,2,1:T(4,128)(2,1)S(1)} %copy.164), channel_id=1, source_target_pairs={{64,0},{72,8},{80,16},{88,24},{96,32},{104,40},{112,48},{120,56},{... | collective-permute-start | bytes 1179656 | tf_op jit(solution)/shard_map/ppermute | solution.py:13
  35.2 826.9 %all-to-all-start = ((s32[8,3,4]{2,1,0:T(4,128)}), s32[8,3,4]{2,1,0:T(4,128)S(1)}, u32[]{:S(2)}, u32[]{:S(2)}) async-start(s32[8,3,4]{2,1,0:T(4,128)} %stack.2), calls=%async_computation | async-start | bytes 32768 | tf_op jit(solution)/shard_map/all_to_all | solution.py:32
  51.6 67.6 %collective-permute-start.12 = (s32[3,1]{0,1:T(1,128)}, s32[3,1]{0,1:T(1,128)S(1)}, u32[]{:S(2)}, u32[]{:S(2)}) collective-permute-start(s32[3,1]{0,1:T(1,128)} %param.7), channel_id=1, source_target_pairs={{264,0},{272,8},{280,16},{288,24},{296,32},{304,40},{312,48},{320,... | collective-permute-start | bytes 44 | tf_op jit(solution)/shard_map/ppermute | solution.py:13
  54.2 67.9 %collective-permute-start.13 = (s32[3,1]{0,1:T(1,128)}, s32[3,1]{0,1:T(1,128)S(1)}, u32[]{:S(2)}, u32[]{:S(2)}) collective-permute-start(s32[3,1]{0,1:T(1,128)} %param.7), channel_id=1, source_target_pairs={{312,0},{320,8},{328,16},{336,24},{344,32},{352,40},{360,48},{368,... | collective-permute-start | bytes 44 | tf_op jit(solution)/shard_map/ppermute | solution.py:13
  119.2 10.4 collective-permute-start.14
  122.1 14.8 %collective-permute-start.15 = (s32[3,1]{0,1:T(1,128)}, s32[3,1]{0,1:T(1,128)S(1)}, u32[]{:S(2)}, u32[]{:S(2)}) collective-permute-start(s32[3,1]{0,1:T(1,128)} %param.7), channel_id=1, source_target_pairs={{328,0},{336,8},{344,16},{352,24},{360,32},{368,40},{376,48},{384,... | collective-permute-start | bytes 44 | tf_op jit(solution)/shard_map/ppermute | solution.py:13
  129.6 12.5 %collective-permute-start.16 = (s32[3,1]{0,1:T(1,128)}, s32[3,1]{0,1:T(1,128)S(1)}, u32[]{:S(2)}, u32[]{:S(2)}) collective-permute-start(s32[3,1]{0,1:T(1,128)} %param.7), channel_id=1, source_target_pairs={{376,0},{384,8},{392,16},{400,24},{408,32},{416,40},{424,48},{432,... | collective-permute-start | bytes 44 | tf_op jit(solution)/shard_map/ppermute | solution.py:13
  137.0 15.2 %collective-permute-start.17 = (s32[3,1]{0,1:T(1,128)}, s32[3,1]{0,1:T(1,128)S(1)}, u32[]{:S(2)}, u32[]{:S(2)}) collective-permute-start(s32[3,1]{0,1:T(1,128)} %param.7), channel_id=1, source_target_pairs={{384,0},{392,8},{400,16},{408,24},{416,32},{424,40},{432,48},{440,... | collective-permute-start | bytes 44 | tf_op jit(solution)/shard_map/ppermute | solution.py:13
  142.1 14.6 %collective-permute-start.18 = (s32[3,1]{0,1:T(1,128)}, s32[3,1]{0,1:T(1,128)S(1)}, u32[]{:S(2)}, u32[]{:S(2)}) collective-permute-start(s32[3,1]{0,1:T(1,128)} %param.7), channel_id=1, source_target_pairs={{392,0},{400,8},{408,16},{416,24},{424,32},{432,40},{440,48},{448,... | collective-permute-start | bytes 44 | tf_op jit(solution)/shard_map/ppermute | solution.py:13
  152.1 11.9 %collective-permute-start.19 = (s32[3,1]{0,1:T(1,128)}, s32[3,1]{0,1:T(1,128)S(1)}, u32[]{:S(2)}, u32[]{:S(2)}) collective-permute-start(s32[3,1]{0,1:T(1,128)} %param.7), channel_id=1, source_target_pairs={{440,0},{448,8},{456,16},{464,24},{472,32},{480,40},{488,48},{496,... | collective-permute-start | bytes 44 | tf_op jit(solution)/shard_map/ppermute | solution.py:13
  156.7 11.8 collective-permute-start.2
  164.0 10.4 collective-permute-start.20
  168.5 9.8 collective-permute-start.21
  178.3 10.4 collective-permute-start.3
  182.5 15.3 %collective-permute-start.4 = (s32[3,1]{0,1:T(1,128)}, s32[3,1]{0,1:T(1,128)S(1)}, u32[]{:S(2)}, u32[]{:S(2)}) collective-permute-start(s32[3,1]{0,1:T(1,128)} %param.7), channel_id=1, source_target_pairs={{120,0},{128,8},{136,16},{144,24},{152,32},{160,40},{168,48},{176,... | collective-permute-start | bytes 44 | tf_op jit(solution)/shard_map/ppermute | solution.py:13
  188.8 14.8 %collective-permute-start.5 = (s32[3,1]{0,1:T(1,128)}, s32[3,1]{0,1:T(1,128)S(1)}, u32[]{:S(2)}, u32[]{:S(2)}) collective-permute-start(s32[3,1]{0,1:T(1,128)} %param.7), channel_id=1, source_target_pairs={{128,0},{136,8},{144,16},{152,24},{160,32},{168,40},{176,48},{184,... | collective-permute-start | bytes 44 | tf_op jit(solution)/shard_map/ppermute | solution.py:13
  197.8 13.7 %collective-permute-start.6 = (s32[3,1]{0,1:T(1,128)}, s32[3,1]{0,1:T(1,128)S(1)}, u32[]{:S(2)}, u32[]{:S(2)}) collective-permute-start(s32[3,1]{0,1:T(1,128)} %param.7), channel_id=1, source_target_pairs={{136,0},{144,8},{152,16},{160,24},{168,32},{176,40},{184,48},{192,... | collective-permute-start | bytes 44 | tf_op jit(solution)/shard_map/ppermute | solution.py:13
  203.6 13.4 %collective-permute-start.7 = (s32[3,1]{0,1:T(1,128)}, s32[3,1]{0,1:T(1,128)S(1)}, u32[]{:S(2)}, u32[]{:S(2)}) collective-permute-start(s32[3,1]{0,1:T(1,128)} %param.7), channel_id=1, source_target_pairs={{184,0},{192,8},{200,16},{208,24},{216,32},{224,40},{232,48},{240,... | collective-permute-start | bytes 44 | tf_op jit(solution)/shard_map/ppermute | solution.py:13
  211.5 9.5 collective-permute-start.8
  217.0 8.9 collective-permute-start.9
  225.9 8.6 collective-permute-start.24
  229.0 11.3 collective-permute-start.25
  234.5 11.9 %collective-permute-start.26 = (s32[3,4]{0,1:T(4,128)S(1)}, s32[3,4]{0,1:T(4,128)S(1)}, u32[]{:S(2)}, u32[]{:S(2)}) collective-permute-start(s32[3,4]{0,1:T(4,128)S(1)} %copy.140), channel_id=1, source_target_pairs={{72,0},{80,8},{88,16},{96,24},{104,32},{112,40},{120,48},{128,56},... | collective-permute-start | bytes 152 | tf_op jit(solution)/shard_map/ppermute | solution.py:13
  240.4 14.1 %collective-permute-start.27 = (s32[3,4]{0,1:T(4,128)S(1)}, s32[3,4]{0,1:T(4,128)S(1)}, u32[]{:S(2)}, u32[]{:S(2)}) collective-permute-start(s32[3,4]{0,1:T(4,128)S(1)} %copy.140), channel_id=1, source_target_pairs={{120,0},{128,8},{136,16},{144,24},{152,32},{160,40},{168,48},{176,... | collective-permute-start | bytes 152 | tf_op jit(solution)/shard_map/ppermute | solution.py:13
  246.4 15.2 %collective-permute-start.28 = (s32[3,4]{0,1:T(4,128)S(1)}, s32[3,4]{0,1:T(4,128)S(1)}, u32[]{:S(2)}, u32[]{:S(2)}) collective-permute-start(s32[3,4]{0,1:T(4,128)S(1)} %copy.140), channel_id=1, source_target_pairs={{128,0},{136,8},{144,16},{152,24},{160,32},{168,40},{176,48},{184,... | collective-permute-start | bytes 152 | tf_op jit(solution)/shard_map/ppermute | solution.py:13
  254.5 13.6 %collective-permute-start.29 = (s32[3,4]{0,1:T(4,128)S(1)}, s32[3,4]{0,1:T(4,128)S(1)}, u32[]{:S(2)}, u32[]{:S(2)}) collective-permute-start(s32[3,4]{0,1:T(4,128)S(1)} %copy.140), channel_id=1, source_target_pairs={{136,0},{144,8},{152,16},{160,24},{168,32},{176,40},{184,48},{192,... | collective-permute-start | bytes 152 | tf_op jit(solution)/shard_map/ppermute | solution.py:13
  261.7 11.5 collective-permute-start.30
  268.1 9.4 collective-permute-start.31
  273.2 8.8 collective-permute-start.32
  284.7 9.1 collective-permute-start.35
  287.5 11.7 collective-permute-start.36
  293.8 11.8 collective-permute-start.37
  299.2 12.3 %collective-permute-start.38 = (s32[3,4]{0,1:T(4,128)S(1)}, s32[3,4]{0,1:T(4,128)S(1)}, u32[]{:S(2)}, u32[]{:S(2)}) collective-permute-start(s32[3,4]{0,1:T(4,128)S(1)} %copy.140), channel_id=1, source_target_pairs={{328,0},{336,8},{344,16},{352,24},{360,32},{368,40},{376,48},{384,... | collective-permute-start | bytes 152 | tf_op jit(solution)/shard_map/ppermute | solution.py:13
  305.6 13.6 %collective-permute-start.39 = (s32[3,4]{0,1:T(4,128)S(1)}, s32[3,4]{0,1:T(4,128)S(1)}, u32[]{:S(2)}, u32[]{:S(2)}) collective-permute-start(s32[3,4]{0,1:T(4,128)S(1)} %copy.140), channel_id=1, source_target_pairs={{376,0},{384,8},{392,16},{400,24},{408,32},{416,40},{424,48},{432,... | collective-permute-start | bytes 152 | tf_op jit(solution)/shard_map/ppermute | solution.py:13
  311.5 15.1 %collective-permute-start.40 = (s32[3,4]{0,1:T(4,128)S(1)}, s32[3,4]{0,1:T(4,128)S(1)}, u32[]{:S(2)}, u32[]{:S(2)}) collective-permute-start(s32[3,4]{0,1:T(4,128)S(1)} %copy.140), channel_id=1, source_target_pairs={{384,0},{392,8},{400,16},{408,24},{416,32},{424,40},{432,48},{440,... | collective-permute-start | bytes 152 | tf_op jit(solution)/shard_map/ppermute | solution.py:13
  319.2 14.5 %collective-permute-start.41 = (s32[3,4]{0,1:T(4,128)S(1)}, s32[3,4]{0,1:T(4,128)S(1)}, u32[]{:S(2)}, u32[]{:S(2)}) collective-permute-start(s32[3,4]{0,1:T(4,128)S(1)} %copy.140), channel_id=1, source_target_pairs={{392,0},{400,8},{408,16},{416,24},{424,32},{432,40},{440,48},{448,... | collective-permute-start | bytes 152 | tf_op jit(solution)/shard_map/ppermute | solution.py:13
  326.6 12.1 %collective-permute-start.42 = (s32[3,4]{0,1:T(4,128)S(1)}, s32[3,4]{0,1:T(4,128)S(1)}, u32[]{:S(2)}, u32[]{:S(2)}) collective-permute-start(s32[3,4]{0,1:T(4,128)S(1)} %copy.140), channel_id=1, source_target_pairs={{440,0},{448,8},{456,16},{464,24},{472,32},{480,40},{488,48},{496,... | collective-permute-start | bytes 152 | tf_op jit(solution)/shard_map/ppermute | solution.py:13
  333.7 10.3 collective-permute-start.43
  338.7 9.7 collective-permute-start.44
  348.4 60.9 %collective-permute-start.49 = (bf16[3,4,128,128]{3,0,2,1:T(4,128)(2,1)S(1)}, bf16[3,4,128,128]{3,0,2,1:T(4,128)(2,1)S(1)}, u32[]{:S(2)}, u32[]{:S(2)}) collective-permute-start(bf16[3,4,128,128]{3,0,2,1:T(4,128)(2,1)S(1)} %copy.164), channel_id=1, source_target_pairs={{72,0},{80,8},{88,16},{96,24},{104,32},{112,40},{120,48},{128,56},... | collective-permute-start | bytes 1179656 | tf_op jit(solution)/shard_map/ppermute | solution.py:13
  352.5 117.6 %collective-permute-start.50 = (bf16[3,4,128,128]{3,0,2,1:T(4,128)(2,1)S(1)}, bf16[3,4,128,128]{3,0,2,1:T(4,128)(2,1)S(1)}, u32[]{:S(2)}, u32[]{:S(2)}) collective-permute-start(bf16[3,4,128,128]{3,0,2,1:T(4,128)(2,1)S(1)} %copy.164), channel_id=1, source_target_pairs={{120,0},{128,8},{136,16},{144,24},{152,32},{160,40},{168,48},{176,... | collective-permute-start | bytes 1179656 | tf_op jit(solution)/shard_map/ppermute | solution.py:13
  358.9 113.2 %collective-permute-start.51 = (bf16[3,4,128,128]{3,0,2,1:T(4,128)(2,1)S(1)}, bf16[3,4,128,128]{3,0,2,1:T(4,128)(2,1)S(1)}, u32[]{:S(2)}, u32[]{:S(2)}) collective-permute-start(bf16[3,4,128,128]{3,0,2,1:T(4,128)(2,1)S(1)} %copy.164), channel_id=1, source_target_pairs={{128,0},{136,8},{144,16},{152,24},{160,32},{168,40},{176,48},{184,... | collective-permute-start | bytes 1179656 | tf_op jit(solution)/shard_map/ppermute | solution.py:13
  367.8 119.7 %collective-permute-start.52 = (bf16[3,4,128,128]{3,0,2,1:T(4,128)(2,1)S(1)}, bf16[3,4,128,128]{3,0,2,1:T(4,128)(2,1)S(1)}, u32[]{:S(2)}, u32[]{:S(2)}) collective-permute-start(bf16[3,4,128,128]{3,0,2,1:T(4,128)(2,1)S(1)} %copy.164), channel_id=1, source_target_pairs={{136,0},{144,8},{152,16},{160,24},{168,32},{176,40},{184,48},{192,... | collective-permute-start | bytes 1179656 | tf_op jit(solution)/shard_map/ppermute | solution.py:13
  372.5 157.3 %collective-permute-start.53 = (bf16[3,4,128,128]{3,0,2,1:T(4,128)(2,1)S(1)}, bf16[3,4,128,128]{3,0,2,1:T(4,128)(2,1)S(1)}, u32[]{:S(2)}, u32[]{:S(2)}) collective-permute-start(bf16[3,4,128,128]{3,0,2,1:T(4,128)(2,1)S(1)} %copy.164), channel_id=1, source_target_pairs={{184,0},{192,8},{200,16},{208,24},{216,32},{224,40},{232,48},{240,... | collective-permute-start | bytes 1179656 | tf_op jit(solution)/shard_map/ppermute | solution.py:13
  409.3 196.5 %collective-permute-start.54 = (bf16[3,4,128,128]{3,0,2,1:T(4,128)(2,1)S(1)}, bf16[3,4,128,128]{3,0,2,1:T(4,128)(2,1)}, u32[]{:S(2)}, u32[]{:S(2)}) collective-permute-start(bf16[3,4,128,128]{3,0,2,1:T(4,128)(2,1)S(1)} %copy.164), channel_id=1, source_target_pairs={{192,0},{200,8},{208,16},{216,24},{224,32},{232,40},{240,48},{248,... | collective-permute-start | bytes 1179656 | tf_op jit(solution)/shard_map/ppermute | solution.py:13
  470.1 150.7 %collective-permute-start.55 = (bf16[3,4,128,128]{3,0,2,1:T(4,128)(2,1)S(1)}, bf16[3,4,128,128]{3,0,2,1:T(4,128)(2,1)}, u32[]{:S(2)}, u32[]{:S(2)}) collective-permute-start(bf16[3,4,128,128]{3,0,2,1:T(4,128)(2,1)S(1)} %copy.164), channel_id=1, source_target_pairs={{200,0},{208,8},{216,16},{224,24},{232,32},{240,40},{248,48},{256,... | collective-permute-start | bytes 1179656 | tf_op jit(solution)/shard_map/ppermute | solution.py:13
  472.1 162.0 %collective-permute-start.56 = (bf16[3,4,128,128]{3,0,2,1:T(4,128)(2,1)S(1)}, bf16[3,4,128,128]{3,0,2,1:T(4,128)(2,1)}, u32[]{:S(2)}, u32[]{:S(2)}) collective-permute-start(bf16[3,4,128,128]{3,0,2,1:T(4,128)(2,1)S(1)} %copy.164), channel_id=1, source_target_pairs={{248,0},{256,8},{264,16},{272,24},{280,32},{288,40},{296,48},{304,... | collective-permute-start | bytes 1179656 | tf_op jit(solution)/shard_map/ppermute | solution.py:13
  487.5 153.6 %collective-permute-start.57 = (bf16[3,4,128,128]{3,0,2,1:T(4,128)(2,1)S(1)}, bf16[3,4,128,128]{3,0,2,1:T(4,128)(2,1)}, u32[]{:S(2)}, u32[]{:S(2)}) collective-permute-start(bf16[3,4,128,128]{3,0,2,1:T(4,128)(2,1)S(1)} %copy.164), channel_id=1, source_target_pairs={{256,0},{264,8},{272,16},{280,24},{288,32},{296,40},{304,48},{312,... | collective-permute-start | bytes 1179656 | tf_op jit(solution)/shard_map/ppermute | solution.py:13
  529.8 119.0 %collective-permute-start.58 = (bf16[3,4,128,128]{3,0,2,1:T(4,128)(2,1)S(1)}, bf16[3,4,128,128]{3,0,2,1:T(4,128)(2,1)}, u32[]{:S(2)}, u32[]{:S(2)}) collective-permute-start(bf16[3,4,128,128]{3,0,2,1:T(4,128)(2,1)S(1)} %copy.164), channel_id=1, source_target_pairs={{264,0},{272,8},{280,16},{288,24},{296,32},{304,40},{312,48},{320,... | collective-permute-start | bytes 1179656 | tf_op jit(solution)/shard_map/ppermute | solution.py:13
  605.8 57.3 %collective-permute-start.59 = (bf16[3,4,128,128]{3,0,2,1:T(4,128)(2,1)S(1)}, bf16[3,4,128,128]{3,0,2,1:T(4,128)(2,1)}, u32[]{:S(2)}, u32[]{:S(2)}) collective-permute-start(bf16[3,4,128,128]{3,0,2,1:T(4,128)(2,1)S(1)} %copy.164), channel_id=1, source_target_pairs={{312,0},{320,8},{328,16},{336,24},{344,32},{352,40},{360,48},{368,... | collective-permute-start | bytes 1179656 | tf_op jit(solution)/shard_map/ppermute | solution.py:13
  620.9 112.3 %collective-permute-start.60 = (bf16[3,4,128,128]{3,0,2,1:T(4,128)(2,1)S(1)}, bf16[3,4,128,128]{3,0,2,1:T(4,128)(2,1)}, u32[]{:S(2)}, u32[]{:S(2)}) collective-permute-start(bf16[3,4,128,128]{3,0,2,1:T(4,128)(2,1)S(1)} %copy.164), channel_id=1, source_target_pairs={{320,0},{328,8},{336,16},{344,24},{352,32},{360,40},{368,48},{376,... | collective-permute-start | bytes 1179656 | tf_op jit(solution)/shard_map/ppermute | solution.py:13
  634.1 178.1 %collective-permute-start.61 = (bf16[3,4,128,128]{3,0,2,1:T(4,128)(2,1)S(1)}, bf16[3,4,128,128]{3,0,2,1:T(4,128)(2,1)}, u32[]{:S(2)}, u32[]{:S(2)}) collective-permute-start(bf16[3,4,128,128]{3,0,2,1:T(4,128)(2,1)S(1)} %copy.164), channel_id=1, source_target_pairs={{328,0},{336,8},{344,16},{352,24},{360,32},{368,40},{376,48},{384,... | collective-permute-start | bytes 1179656 | tf_op jit(solution)/shard_map/ppermute | solution.py:13
  641.1 175.3 %collective-permute-start.62 = (bf16[3,4,128,128]{3,0,2,1:T(4,128)(2,1)S(1)}, bf16[3,4,128,128]{3,0,2,1:T(4,128)(2,1)}, u32[]{:S(2)}, u32[]{:S(2)}) collective-permute-start(bf16[3,4,128,128]{3,0,2,1:T(4,128)(2,1)S(1)} %copy.164), channel_id=1, source_target_pairs={{376,0},{384,8},{392,16},{400,24},{408,32},{416,40},{424,48},{432,... | collective-permute-start | bytes 1179656 | tf_op jit(solution)/shard_map/ppermute | solution.py:13
  648.8 184.5 %collective-permute-start.63 = (bf16[3,4,128,128]{3,0,2,1:T(4,128)(2,1)S(1)}, bf16[3,4,128,128]{3,0,2,1:T(4,128)(2,1)}, u32[]{:S(2)}, u32[]{:S(2)}) collective-permute-start(bf16[3,4,128,128]{3,0,2,1:T(4,128)(2,1)S(1)} %copy.164), channel_id=1, source_target_pairs={{384,0},{392,8},{400,16},{408,24},{416,32},{424,40},{432,48},{440,... | collective-permute-start | bytes 1179656 | tf_op jit(solution)/shard_map/ppermute | solution.py:13
  663.1 199.7 %collective-permute-start.64 = (bf16[3,4,128,128]{3,0,2,1:T(4,128)(2,1)S(1)}, bf16[3,4,128,128]{3,0,2,1:T(4,128)(2,1)}, u32[]{:S(2)}, u32[]{:S(2)}) collective-permute-start(bf16[3,4,128,128]{3,0,2,1:T(4,128)(2,1)S(1)} %copy.164), channel_id=1, source_target_pairs={{392,0},{400,8},{408,16},{416,24},{424,32},{432,40},{440,48},{448,... | collective-permute-start | bytes 1179656 | tf_op jit(solution)/shard_map/ppermute | solution.py:13
  733.2 129.7 %collective-permute-start.65 = (bf16[3,4,128,128]{3,0,2,1:T(4,128)(2,1)S(1)}, bf16[3,4,128,128]{3,0,2,1:T(4,128)(2,1)}, u32[]{:S(2)}, u32[]{:S(2)}) collective-permute-start(bf16[3,4,128,128]{3,0,2,1:T(4,128)(2,1)S(1)} %copy.164), channel_id=1, source_target_pairs={{440,0},{448,8},{456,16},{464,24},{472,32},{480,40},{488,48},{496,... | collective-permute-start | bytes 1179656 | tf_op jit(solution)/shard_map/ppermute | solution.py:13
  812.2 105.0 %collective-permute-start.66 = (bf16[3,4,128,128]{3,0,2,1:T(4,128)(2,1)S(1)}, bf16[3,4,128,128]{3,0,2,1:T(4,128)(2,1)}, u32[]{:S(2)}, u32[]{:S(2)}) collective-permute-start(bf16[3,4,128,128]{3,0,2,1:T(4,128)(2,1)S(1)} %copy.164), channel_id=1, source_target_pairs={{448,0},{456,8},{464,16},{472,24},{480,32},{488,40},{496,48},{504,... | collective-permute-start | bytes 1179656 | tf_op jit(solution)/shard_map/ppermute | solution.py:13
  816.4 111.4 %collective-permute-start.67 = (bf16[3,4,128,128]{3,0,2,1:T(4,128)(2,1)S(1)}, bf16[3,4,128,128]{3,0,2,1:T(4,128)(2,1)}, u32[]{:S(2)}, u32[]{:S(2)}) collective-permute-start(bf16[3,4,128,128]{3,0,2,1:T(4,128)(2,1)S(1)} %copy.164), channel_id=1, source_target_pairs={{456,0},{464,8},{472,16},{480,24},{488,32},{496,40},{504,48},{0,56... | collective-permute-start | bytes 1179656 | tf_op jit(solution)/shard_map/ppermute | solution.py:13
  833.3 112.1 %collective-permute-start.68 = (bf16[3,4,128,128]{3,0,2,1:T(4,128)(2,1)S(1)}, bf16[3,4,128,128]{3,0,2,1:T(4,128)(2,1)}, u32[]{:S(2)}, u32[]{:S(2)}) collective-permute-start(bf16[3,4,128,128]{3,0,2,1:T(4,128)(2,1)S(1)} %copy.164), channel_id=1, source_target_pairs={{504,0},{0,8},{8,16},{16,24},{24,32},{32,40},{40,48},{48,56},{56,6... | collective-permute-start | bytes 1179656 | tf_op jit(solution)/shard_map/ppermute | solution.py:13
  (36 other events, 10823.2 us)
Sparse Core Ops, SparseCore 0:
  10.6 81.3 all-gather.2
